TPU v7x, 32 devices: a whole 2x2x4 slice. The times are simulated.
32 devices in a mesh: obs: 16 (over z, y, x), chan: 2 (over core).
Axes of the slice: x: 2, y: 2, z: 4, core: 2. Of those that a mesh axis runs over, the one named last changes fastest.
Arguments:
- observed: bfloat16 [16384, 128], P('obs', 'chan'), may hold values from -6 to 6
- predictors: bfloat16 [16384, 128], P('obs'), may hold values from -6 to 6
- cells: int32 [16384], P('obs'), may hold values from 0 to 65535, as said below
- columns: bfloat16 [65536, 274], P('obs'), may hold values from -6 to 6
- obs_error: float32 [128], P('chan'), may hold values from 0.5 to 2
- w_col: bfloat16 [274, 1024], P(None, 'chan'), may hold values from -0.3125 to 0.3125
- w_pred: bfloat16 [128, 1024], P(None, 'chan'), may hold values from -0.3125 to 0.3125
- w_mid: bfloat16 [1024, 1024], P(None, 'chan'), may hold values from -0.1875 to 0.1875
- w_out: bfloat16 [1024, 128], P('chan'), may hold values from -0.375 to 0.375
Outputs:
- departures: float32 [16384, 128], P('obs', 'chan')
Inputs may be any that keep to these rules, and one draw needn't show every extreme that they name: `cells`: the owner of cell c is c // 4096. Among the 1024 footprints of one index of obs, at most 160 fall on any one owner; in every draw 1 owners receive exactly 160 from every index of obs.
All inputs are finite; a program needn't handle non-finite values.
Results may differ from a plain program's by a relative error of at most 0.0028.
Values may be sent and summed in bfloat16 or wider, within the bound.
A program may use at most 64 MiB of HBM per device.

v0:
```python
import jax
import jax.numpy as jnp
from jax import lax
from jax.sharding import PartitionSpec as P


def evolve_whole(column, pred_rows, w_col, w_pred, w_mid, w_out):
    first = jnp.dot(column, w_col, preferred_element_type=jnp.float32)
    first = first + jnp.dot(pred_rows, w_pred, preferred_element_type=jnp.float32)
    hidden = jax.nn.silu(first).astype(jnp.bfloat16)
    upper = jax.nn.silu(jnp.dot(hidden, w_mid, preferred_element_type=jnp.float32)).astype(
        jnp.bfloat16
    )
    return jnp.dot(upper, w_out, preferred_element_type=jnp.float32)


def on_device(observed, predictors, cells, columns, obs_error, w_col, w_pred, w_mid, w_out):
    shards = lax.axis_size("obs")
    count_rows = cells.shape[0]
    cell_dev = columns.shape[0]
    cap = 5 * count_rows // (2 * shards)
    owner = cells // cell_dev
    local = cells % cell_dev
    one_hot = (owner[:, None] == jnp.arange(shards, dtype=jnp.int32)[None, :]).astype(jnp.int32)
    before = jnp.cumsum(one_hot, axis=0) - one_hot
    rank = jnp.sum(before * one_hot, axis=1)
    target = owner * cap + rank
    send_cell = jnp.zeros((shards * cap,), jnp.int32).at[target].set(local).reshape(shards, cap)
    width = (cap + 1) // 2
    w_col, w_pred, w_mid, w_out = (
        lax.all_gather(w_col, "chan", axis=1, tiled=True),
        lax.all_gather(w_pred, "chan", axis=1, tiled=True),
        lax.all_gather(w_mid, "chan", axis=1, tiled=True),
        lax.all_gather(w_out, "chan", axis=0, tiled=True),
    )
    core = lax.axis_index("chan")

    def own_half(values):
        return lax.dynamic_slice_in_dim(values, core * width, width, 1)

    slot_cell = own_half(send_cell)
    placed = jnp.zeros((shards * cap, predictors.shape[1]), jnp.bfloat16).at[target].set(predictors)
    slot_pred = own_half(placed.reshape(shards, cap, predictors.shape[1]))
    got_pred = lax.all_to_all(slot_pred, "obs", split_axis=0, concat_axis=0, tiled=True)
    got_cell = lax.all_to_all(slot_cell, "obs", split_axis=0, concat_axis=0, tiled=True)
    count = got_cell.shape[1]
    column = jnp.take(columns, got_cell.reshape(-1), axis=0)
    radiance = evolve_whole(
        column, got_pred.reshape(-1, got_pred.shape[2]), w_col, w_pred, w_mid, w_out
    )
    radiance = radiance.reshape(shards, count, radiance.shape[1])
    slot_rad = lax.all_to_all(radiance, "obs", split_axis=0, concat_axis=0, tiled=True)
    mine = lax.all_to_all(slot_rad, "chan", split_axis=2, concat_axis=1, tiled=True)
    evolved = jnp.take(mine.reshape(shards * cap, mine.shape[2]), target, axis=0)
    return (observed.astype(jnp.float32) - evolved) / obs_error[None, :]


def solution(mesh):
    return jax.shard_map(
        on_device,
        mesh=mesh,
        in_specs=(
            P("obs", "chan"),
            P("obs", None),
            P("obs"),
            P("obs", None),
            P("chan"),
            P(None, "chan"),
            P(None, "chan"),
            P(None, "chan"),
            P("chan", None),
        ),
        out_specs=P("obs", "chan"),
        check_vma=False,
    )
```

profile of v0, /device:TPU:0, one launch (start us, length us, event | category | flops | bytes accessed | tf_op | source)
XLA Modules:
  0.0 120.3 jit_solution(11798314648579643925)
XLA Ops:
  6.5 0.7 all-gather.2.cloned.1.call-update
  7.3 0.7 add_select_fusion
  8.0 4.5 %reduce-window.6 = s32[16,8,128]{2,1,0:T(8,128)S(1)} reduce-window(s32[16,8,128]{2,1,0:T(8,128)S(1)} %fusion.11, s32[]{:T(128)} %constant.65.clone.1), window={size=1x1x128 pad=0_0x0_0x127_0}, to_apply=%region_0.1 | reduce-window | flops 2080768 | bytes 131076 | tf_op jit(solution)/shard_map/reduce-window
  13.0 4.3 %scatter_custom_fusion = s32[2560]{0:T(1024)S(1)} fusion(s32[1024]{0:T(1024)S(1)} %get-tuple-element.6, s32[1024]{0:T(1024)S(1)} %get-tuple-element.7, s32[]{:T(128)} %constant.65.clone.1), kind=kCustom, calls=%fused_computation.29 | custom fusion | bytes 10244 | tf_op jit(solution)/shard_map/scatter | solution.py:28
  17.4 0.7 constant_dynamic-slice_fusion.1
  18.0 8.3 %all-to-all-start = ((s32[16,1,80]{2,1,0:T(1,128)}), s32[16,1,80]{2,1,0:T(1,128)S(1)}, u32[]{:S(2)}, u32[]{:S(2)}) async-start(s32[16,1,80]{2,1,0:T(1,128)} %bitcast.3), calls=%async_computation | async-start | bytes 16384 | tf_op jit(solution)/shard_map/all_to_all | solution.py:45
  26.4 3.7 %scatter_custom_fusion.1 = bf16[2560,128]{1,0:T(8,128)(2,1)S(1)} fusion(s32[1024]{0:T(1024)S(1)} %get-tuple-element.6, bf16[1024,128]{1,0:T(8,128)(2,1)} %param.10, bf16[]{:T(256)} %constant.76.clone.1), kind=kCustom, calls=%fused_computation.12 | custom fusion | bytes 655872 | tf_op jit(solution)/shard_map/scatter | solution.py:42
  30.1 3.7 %all_gather.13 = bf16[128,1024]{1,0:T(8,128)(2,1)} all-gather(bf16[128,512]{1,0:T(8,128)(2,1)} %param.15), channel_id=1, replica_groups=mesh['obs'=16,'chan'=2] {'chan'}, dimensions={1}, use_global_device_ids=true | all-gather | bytes 393216 | tf_op jit(solution)/shard_map/all_gather | solution.py:32
  33.8 0.8 constant_dynamic-slice_fusion
  34.5 5.6 %all_gather.12 = bf16[274,1024]{1,0:T(8,128)(2,1)} all-gather(bf16[274,512]{1,0:T(8,128)(2,1)} %param.14), channel_id=1, replica_groups=mesh['obs'=16,'chan'=2] {'chan'}, dimensions={1}, use_global_device_ids=true | all-gather | bytes 841728 | tf_op jit(solution)/shard_map/all_gather | solution.py:31
  40.1 3.5 %all_gather.15 = bf16[1024,128]{1,0:T(8,128)(2,1)} all-gather(bf16[512,128]{1,0:T(8,128)(2,1)} %param.17), channel_id=1, replica_groups=mesh['obs'=16,'chan'=2] {'chan'}, dimensions={0}, use_global_device_ids=true | all-gather | bytes 393216 | tf_op jit(solution)/shard_map/all_gather | solution.py:34
  43.6 3.3 %copy.33 = bf16[4096,274]{1,0:T(8,128)(2,1)S(1)} copy(bf16[4096,274]{0,1:T(8,128)(2,1)} %param.12) | data formatting | bytes 4489216 | tf_op args[3]
  46.9 6.9 %all-to-all-start.1 = ((bf16[16,80,128]{2,1,0:T(8,128)(2,1)}), bf16[16,80,128]{2,1,0:T(8,128)(2,1)S(1)}, u32[]{:S(2)}, u32[]{:S(2)}) async-start(bf16[16,80,128]{2,1,0:T(8,128)(2,1)} %constant_dynamic-slice_fusion), calls=%async_computation.1 | async-start | bytes 655360 | tf_op jit(solution)/shard_map/all_to_all | solution.py:44
  54.4 0.7 reduce.7
  55.2 4.6 %gather_fusion = bf16[1280,274]{1,0:T(8,128)(2,1)} fusion(bf16[4096,274]{1,0:T(8,128)(2,1)S(1)} %copy.33, s32[2048]{0:T(1024)S(1)} %pad_clamp_fusion), kind=kCustom, calls=%fused_computation | custom fusion | bytes 1408000 | tf_op jit(solution)/shard_map/jit(_take)/gather | solution.py:47
  59.9 5.3 %fusion.2 = f32[1280,1024]{1,0:T(8,128)} fusion(bf16[274,1024]{1,0:T(8,128)(2,1)} %all_gather.12, bf16[1280,274]{1,0:T(8,128)(2,1)} %gather_fusion, pred[1280]{0:T(1024)(128)(4,1)S(1)} %compare_and_fusion), kind=kOutput, calls=%fused_computation.8 | convolution fusion | flops 718625280 | bytes 6506752 | tf_op jit(solution)/shard_map/dot_general | solution.py:8
  65.7 9.5 %fusion.1 = f32[1280,1024]{1,0:T(8,128)} fusion(bf16[1024,1024]{1,0:T(8,128)(2,1)} %all-gather.2.cloned.1.call-done, f32[1280,1024]{1,0:T(8,128)} %fusion.2, bf16[1280,128]{1,0:T(8,128)(2,1)S(1)} %bitcast.36, bf16[128,1024]{1,0:T(8,128)(2,1)S(1)} %copy-done), kind=kOutput, calls=%fused_computation.7 | convolution fusion | flops 3027763200 | bytes 13172736 | tf_op jit(solution)/shard_map/dot_general | solution.py:11
  75.2 4.8 %fusion = f32[1280,128]{1,0:T(8,128)} fusion(bf16[1024,128]{1,0:T(8,128)(2,1)S(1)} %copy-done.1, f32[1280,1024]{1,0:T(8,128)} %fusion.1), kind=kOutput, calls=%fused_computation.6 | convolution fusion | flops 342097920 | bytes 6160384 | tf_op jit(solution)/shard_map/dot_general | solution.py:14
  80.1 6.4 %all-to-all-start.2 = ((f32[16,80,128]{2,1,0:T(8,128)}), f32[16,80,128]{2,1,0:T(8,128)S(1)}, u32[]{:S(2)}, u32[]{:S(2)}) async-start(f32[16,80,128]{2,1,0:T(8,128)} %bitcast.6), calls=%async_computation.2 | async-start | bytes 1310720 | tf_op jit(solution)/shard_map/all_to_all | solution.py:52
  86.5 17.4 %all-to-all-done.2 = f32[16,80,128]{2,1,0:T(8,128)S(1)} async-done(((f32[16,80,128]{2,1,0:T(8,128)}), f32[16,80,128]{2,1,0:T(8,128)S(1)}, u32[]{:S(2)}, u32[]{:S(2)}) %all-to-all-start.2) | async-done | bytes 655392 | tf_op jit(solution)/shard_map/all_to_all | solution.py:52
  104.4 4.7 %all_to_all.34 = f32[16,80,128]{1,0,2:T(8,128)S(1)} all-to-all(f32[16,80,128]{1,0,2:T(8,128)S(1)} %copy.34), channel_id=1, replica_groups=mesh['obs'=16,'chan'=2] {'chan'}, dimensions={2} | all-to-all | bytes 1310720 | tf_op jit(solution)/shard_map/all_to_all | solution.py:53
  109.1 0.5 copy.36
  109.6 2.8 %gather_fusion.1 = f32[1024,64]{1,0:T(8,128)S(1)} fusion(f32[2560,64]{1,0:T(8,128)S(1)} %bitcast.33, s32[1024]{0:T(1024)S(1)} %broadcast_clamp_fusion), kind=kCustom, calls=%fused_computation.1 | custom fusion | bytes 528384 | tf_op jit(solution)/shard_map/jit(_take)/gather | solution.py:54
  112.6 0.8 subtract_divide_fusion
  (31 shorter events, 2.4 us)
Async XLA Ops:
  6.5 59.1 %all-gather.2.cloned.1.call-start = ((), (), s32[]{:S(2)}) async-start(), calls=%async_computation.4 | async-start | bytes 3145728 | tf_op jit(solution)/shard_map/all_gather | solution.py:33
  18.0 28.9 %all-to-all-start = ((s32[16,1,80]{2,1,0:T(1,128)}), s32[16,1,80]{2,1,0:T(1,128)S(1)}, u32[]{:S(2)}, u32[]{:S(2)}) async-start(s32[16,1,80]{2,1,0:T(1,128)} %bitcast.3), calls=%async_computation | async-start | bytes 16384 | tf_op jit(solution)/shard_map/all_to_all | solution.py:45
  46.9 18.8 %all-to-all-start.1 = ((bf16[16,80,128]{2,1,0:T(8,128)(2,1)}), bf16[16,80,128]{2,1,0:T(8,128)(2,1)S(1)}, u32[]{:S(2)}, u32[]{:S(2)}) async-start(bf16[16,80,128]{2,1,0:T(8,128)(2,1)} %constant_dynamic-slice_fusion), calls=%async_computation.1 | async-start | bytes 655360 | tf_op jit(solution)/shard_map/all_to_all | solution.py:44
  59.9 5.8 %copy-start = (bf16[128,1024]{1,0:T(8,128)(2,1)S(1)}, bf16[128,1024]{1,0:T(8,128)(2,1)}, u32[]{:S(2)}) copy-start(bf16[128,1024]{1,0:T(8,128)(2,1)} %all_gather.13) | copy-start | bytes 786436
  65.7 9.6 %copy-start.1 = (bf16[1024,128]{1,0:T(8,128)(2,1)S(1)}, bf16[1024,128]{1,0:T(8,128)(2,1)}, u32[]{:S(2)}) copy-start(bf16[1024,128]{1,0:T(8,128)(2,1)} %all_gather.15) | copy-start | bytes 786436
  80.1 23.8 %all-to-all-start.2 = ((f32[16,80,128]{2,1,0:T(8,128)}), f32[16,80,128]{2,1,0:T(8,128)S(1)}, u32[]{:S(2)}, u32[]{:S(2)}) async-start(f32[16,80,128]{2,1,0:T(8,128)} %bitcast.6), calls=%async_computation.2 | async-start | bytes 1310720 | tf_op jit(solution)/shard_map/all_to_all | solution.py:52
  104.4 8.3 %copy-start.2 = (bf16[1024,64]{0,1:T(8,128)(2,1)S(1)}, bf16[1024,64]{0,1:T(8,128)(2,1)}, u32[]{:S(2)}) copy-start(bf16[1024,64]{0,1:T(8,128)(2,1)} %param.9) | copy-start | bytes 393220
  104.4 8.3 %copy-start.3 = (f32[64]{0:T(128)S(1)}, f32[64]{0:T(128)}, u32[]{:S(2)}) copy-start(f32[64]{0:T(128)} %param.13) | copy-start | bytes 772
Sparse Core Ops, SparseCore 0:
  8.9 13.2 all-gather.1
where the time goes:
time: 121 us; the launch traced here: 120 us
  local copies, waits for them, and re-layouts  22.4 us (19%)
  starting transfers between devices  21.7 us (18%)
  matrix products  19.7 us (16%)
  waiting for transfers between devices  18.6 us (15%)
  blocking collectives  17.5 us (14%)
  between operations  13.6 us (11%)
  other arithmetic  6.89 us (6%)
    all_to_all x1, waiting for transfers between devices, on_device(): lax.all_to_all(radiance, 'obs', split_axis=0, concat_axis=0, tiled=True)  17.4 us
    dot_general x1, matrix products, evolve_whole(): jnp.dot(hidden, w_mid, preferred_element_type=jnp.float32)  9.55 us
    all_to_all x1, starting transfers between devices, on_device(): lax.all_to_all(slot_cell, 'obs', split_axis=0, concat_axis=0, tiled=True)  8.31 us
    all_to_all x1, starting transfers between devices, on_device(): lax.all_to_all(slot_pred, 'obs', split_axis=0, concat_axis=0, tiled=True)  6.93 us
    all_to_all x1, starting transfers between devices, on_device(): lax.all_to_all(radiance, 'obs', split_axis=0, concat_axis=0, tiled=True)  6.42 us
    all_gather x1, blocking collectives, on_device(): lax.all_gather(w_col, 'chan', axis=1, tiled=True)  5.58 us
    dot_general x1, matrix products, evolve_whole(): first = jnp.dot(column, w_col, preferred_element_type=jnp.float32)  5.3 us
    dot_general x1, matrix products, evolve_whole(): return jnp.dot(upper, w_out, preferred_element_type=jnp.float32)  4.83 us
  transfers between devices with their start and end apart: 4, of which 2 were waited for; matrix products, arithmetic and copies ran while one was open for 25% of the time, Pallas kernels for 0%

commit v1 on v0

v1 whole, which is shorter than its diff:
```python
import functools

import jax
import jax.numpy as jnp
from jax import lax
from jax.experimental import pallas as pl
from jax.experimental.pallas import tpu as pltpu
from jax.sharding import PartitionSpec as P

MESH = pl.DeviceIdType.MESH
LANES = 128
PACK = 24
F32 = jnp.float32
BF16 = jnp.bfloat16


def silu(v):
    h = v * 0.5
    return (h + h * jnp.tanh(h)).astype(BF16)


def dot(a, b):
    return jnp.dot(a, b, preferred_element_type=F32)


def kernel(
    n, slots,
    cells, pred, observed, err, columns, wc, wp, wm, wo,
    out,
    cellv, colv, tab, stage, idx_send, idx_recv, idx_s, sendbuf, recv, tcol, acc,
    predv, obsv, errv, wc_own, wc_oth, wp_own, wp_oth, wm_own, wm_oth, wo_own, wo_oth,
    rem32, w2_own, w2_oth, ev_send, ev_recv,
    in_sem, idx_ssem, idx_rsem, col_ssem, col_rsem, fwd_ssem, fwd_rsem, w_ssem, w_rsem,
    ev_ssem, ev_rsem, smem_sem,
):
    me = lax.axis_index("obs")
    core = lax.axis_index("chan")
    other = 1 - core
    count = cells.shape[1]
    half = count // 2
    cf, cell_dev = columns.shape
    main = 2 * LANES
    extra = cf - main
    groups = slots // 16

    loads = [
        pltpu.make_async_copy(src, dst, in_sem.at[i])
        for i, (src, dst) in enumerate(
            [
                (cells, cellv),
                (columns, colv),
                (pred.at[pl.ds(core * half, half)], predv),
                (observed, obsv),
                (err, errv),
                (wc, wc_own),
                (wp, wp_own),
                (wm, wm_own),
                (wo, wo_own),
            ]
        )
    ]
    for load in loads:
        load.start()

    barrier = pltpu.get_barrier_semaphore()

    @pl.loop(1, n)
    def _(t):
        pl.semaphore_signal(
            barrier, inc=1, device_id=(lax.rem(me + t, n), core), device_id_type=MESH
        )

    pl.semaphore_signal(barrier, inc=1, device_id=(me, other), device_id_type=MESH)

    loads[0].wait()
    cell = cellv[...]
    owner = cell >> (cell_dev.bit_length() - 1)
    local = cell & (cell_dev - 1)
    hot = (owner == lax.broadcasted_iota(jnp.int32, (n, count), 0)).astype(F32)
    blocks = count // LANES
    cut = [hot[:, b * LANES : (b + 1) * LANES] for b in range(blocks)]
    upto = (
        lax.broadcasted_iota(jnp.int32, (LANES, LANES), 0)
        <= lax.broadcasted_iota(jnp.int32, (LANES, LANES), 1)
    )
    upto = upto.astype(F32).astype(BF16)
    inside = dot(jnp.concatenate(cut, axis=0).astype(BF16), upto)
    run = jnp.zeros((n, 1), F32)
    ranks = []
    for b in range(blocks):
        part = inside[b * n : (b + 1) * n]
        before = part - cut[b] + run
        ranks.append(jnp.sum(before * cut[b], axis=0, keepdims=True))
        run = run + part[:, LANES - 1 : LANES]
    rank = jnp.concatenate(ranks, axis=1).astype(jnp.int32)
    side = rank & 1
    place = rank >> 1
    mine = hot * (side == core).astype(F32)
    high = (local >> 6).astype(F32)
    low = (local & 63).astype(F32)
    values = jnp.concatenate([mine * high, mine * low], axis=0).astype(BF16)
    at = (place == lax.broadcasted_iota(jnp.int32, (LANES, count), 0)).astype(F32).astype(BF16)
    asked = lax.dot_general(values, at, (((1,), (1,)), ((), ())), preferred_element_type=F32)
    asked = (asked[:n] * 64.0 + asked[n:]).astype(jnp.int32) & (cell_dev - 1)
    for o in range(n):
        idx_send[o] = asked[o : o + 1]

    pl.semaphore_wait(barrier, n)

    def idx_copy(t):
        return pltpu.make_async_remote_copy(
            src_ref=idx_send.at[lax.rem(me + t, n)],
            dst_ref=idx_recv.at[me],
            send_sem=idx_ssem.at[t],
            recv_sem=idx_rsem.at[t],
            device_id=(lax.rem(me + t, n), core),
            device_id_type=MESH,
        )

    @pl.loop(1, n)
    def _(t):
        idx_copy(t).start()

    swaps = [
        pltpu.make_async_remote_copy(
            src_ref=src, dst_ref=dst, send_sem=w_ssem.at[i], recv_sem=w_rsem.at[i],
            device_id=(me, other), device_id_type=MESH,
        )
        for i, (src, dst) in enumerate([(wc, wc_oth), (wp, wp_oth), (wm, wm_oth), (wo, wo_oth)])
    ]
    for swap in swaps:
        swap.start()

    idx_recv[me] = idx_send[me]
    target = (owner * (2 * slots) + side * slots + place).astype(F32)
    target = jnp.where(core == 0, target[:, :half], target[:, half:])
    tcol[...] = jnp.transpose(jnp.broadcast_to(target, (LANES, half))).astype(jnp.int32)
    acc[...] = jnp.zeros_like(acc)

    loads[1].wait()
    rows = 256
    unit = (
        lax.broadcasted_iota(jnp.int32, (rows, rows), 0)
        == lax.broadcasted_iota(jnp.int32, (rows, rows), 1)
    )
    unit = unit.astype(F32).astype(BF16)

    def turn(x):
        return lax.dot_general(unit, x, (((1,), (1,)), ((), ())), preferred_element_type=F32)

    @pl.loop(0, cell_dev // rows)
    def _(i):
        at_rows = pl.ds(pl.multiple_of(i * rows, rows), rows)
        tab[at_rows, 0:main] = turn(colv[0:main, at_rows])
        tab[at_rows, main : main + LANES] = jnp.zeros((rows, LANES), F32)
        tab[at_rows, main:cf] = turn(colv[main:cf, at_rows])

    @pl.loop(1, n)
    def _(t):
        idx_copy(t).wait_recv()

    to_smem = pltpu.make_async_copy(idx_recv, idx_s, smem_sem)
    to_smem.start()
    to_smem.wait()

    def gather(asker, dst):
        for k in range(slots):
            stage[k : k + 1, :] = tab[pl.ds(idx_s[asker, 0, k] & (cell_dev - 1), 1), :]
        dst[0:slots, :] = stage[:, 0:LANES].astype(BF16)
        dst[slots : 2 * slots, :] = stage[:, LANES:main].astype(BF16)
        packed = stage[0:16, main:]
        for j in range(1, groups):
            packed = packed + pltpu.roll(stage[16 * j : 16 * j + 16, main:], PACK * j, 1)
        dst[2 * slots : 2 * slots + 16, :] = packed.astype(BF16)

    def col_copy(t):
        asker = lax.rem(me + t, n)
        return pltpu.make_async_remote_copy(
            src_ref=sendbuf.at[asker],
            dst_ref=recv.at[core, me],
            send_sem=col_ssem.at[t],
            recv_sem=col_rsem.at[t],
            device_id=(asker, core),
            device_id_type=MESH,
        )

    def forward(t):
        o = lax.rem(me + n - t, n)
        return pltpu.make_async_remote_copy(
            src_ref=recv.at[core, o],
            dst_ref=recv.at[core, o],
            send_sem=fwd_ssem.at[t],
            recv_sem=fwd_rsem.at[t],
            device_id=(me, other),
            device_id_type=MESH,
        )

    @pl.loop(1, n)
    def _(t):
        asker = lax.rem(me + t, n)
        gather(asker, sendbuf.at[asker])
        col_copy(t).start()

    gather(me, recv.at[core, me])
    forward(0).start()

    for load in loads[2:]:
        load.wait()
    rem32[...] = jnp.zeros_like(rem32)

    def tail(wc_ref, wp_ref, w2):
        rem32[0:extra, :] = wc_ref[main:cf, :].astype(F32)
        w2[0:LANES, :] = rem32[...].astype(BF16)
        w2[LANES:, :] = wp_ref[...]

    tail(wc_own, wp_own, w2_own)
    for swap in swaps:
        swap.wait()
    tail(wc_oth, wp_oth, w2_oth)

    def place_rows(t):
        o = lax.rem(me + n - t, n)
        forward(t).wait_recv()
        sides = []
        for s in range(2):
            packed = recv[s, o, 2 * slots : 2 * slots + 16, :].astype(F32)
            rest = [packed] + [pltpu.roll(packed, LANES - PACK * j, 1) for j in range(1, groups)]
            sides.append(
                jnp.concatenate(
                    [
                        recv[s, o, 0:slots, :],
                        recv[s, o, slots : 2 * slots, :],
                        jnp.concatenate(rest, axis=0).astype(BF16),
                    ],
                    axis=1,
                )
            )
        data = jnp.concatenate(sides, axis=0)
        want = tcol[...] - o * (2 * slots)
        lane = lax.broadcasted_iota(jnp.int32, (half, LANES), 1)
        pick = [
            (want == lane + b).astype(F32).astype(BF16)[:, : min(LANES, 2 * slots - b)]
            for b in range(0, 2 * slots, LANES)
        ]
        acc[...] += dot(jnp.concatenate(pick, axis=1), data)

    @pl.loop(1, n)
    def _(t):
        col_copy(t).wait_recv()
        forward(t).start()
        place_rows(t - 1)

    place_rows(n - 1)

    parts = 2
    chunk = half // parts
    here = pl.ds(pl.multiple_of(core * wc.shape[1], wc.shape[1]), wc.shape[1])
    there = pl.ds(pl.multiple_of(other * wc.shape[1], wc.shape[1]), wc.shape[1])
    chan = out.shape[0]
    spread = jnp.broadcast_to(errv[...], (chan, chan))
    diagonal = (
        lax.broadcasted_iota(jnp.int32, (chan, chan), 0)
        == lax.broadcasted_iota(jnp.int32, (chan, chan), 1)
    )
    error = jnp.sum(jnp.where(diagonal, spread, 0.0), axis=1, keepdims=True)

    def ev_copy(p):
        return pltpu.make_async_remote_copy(
            src_ref=ev_send.at[p], dst_ref=ev_recv.at[p],
            send_sem=ev_ssem.at[p], recv_sem=ev_rsem.at[p],
            device_id=(me, other), device_id_type=MESH,
        )

    for p in range(parts):
        rows_p = slice(p * chunk, (p + 1) * chunk)
        a = acc[rows_p, 0:main].astype(BF16)
        b = jnp.concatenate([acc[rows_p, main:].astype(BF16), predv[rows_p, :]], axis=1)
        h_own = silu(dot(a, wc_own[0:main, :]) + dot(b, w2_own[...]))
        h_oth = silu(dot(a, wc_oth[0:main, :]) + dot(b, w2_oth[...]))
        u_own = silu(dot(h_own, wm_own[here, :]) + dot(h_oth, wm_own[there, :]))
        u_oth = silu(dot(h_own, wm_oth[here, :]) + dot(h_oth, wm_oth[there, :]))
        e = jnp.transpose(dot(u_own, wo_own[...]) + dot(u_oth, wo_oth[...]))
        ev_send[p] = jnp.where(core == 0, e[chan:], e[:chan])
        ev_copy(p).start()
        keep = jnp.where(core == 0, e[:chan], e[chan:])
        at_rows = pl.ds(pl.multiple_of(core * half + p * chunk, chunk), chunk)
        out[:, at_rows] = (obsv[:, at_rows].astype(F32) - keep) / error

    for p in range(parts):
        ev_copy(p).wait_recv()
        at_rows = pl.ds(pl.multiple_of(other * half + p * chunk, chunk), chunk)
        out[:, at_rows] = (obsv[:, at_rows].astype(F32) - ev_recv[p]) / error

    for p in range(parts):
        ev_copy(p).wait_send()
    forward(0).wait_send()

    @pl.loop(1, n)
    def _(t):
        idx_copy(t).wait_send()
        col_copy(t).wait_send()
        forward(t).wait_send()


def on_device(observed, predictors, cells, columns, obs_error, w_col, w_pred, w_mid, w_out):
    n = lax.axis_size("obs")
    count = cells.shape[0]
    cell_dev, cf = columns.shape
    cap = 5 * count // (2 * n)
    slots = (-(-cap // 2) + 15) // 16 * 16
    half = count // 2
    chan = observed.shape[1]
    hid = w_col.shape[1]
    packet = 2 * slots + 16
    dma = pltpu.SemaphoreType.DMA
    vmem = pltpu.VMEM
    any_ = pl.BlockSpec(memory_space=pl.ANY)
    return pl.pallas_call(
        functools.partial(kernel, n, slots),
        out_shape=jax.ShapeDtypeStruct((chan, count), F32),
        in_specs=[any_] * 9,
        out_specs=pl.BlockSpec(memory_space=pltpu.VMEM),
        scratch_shapes=[
            vmem((1, count), jnp.int32),
            vmem((cf, cell_dev), BF16),
            vmem((cell_dev, 3 * LANES), F32),
            vmem((slots, 3 * LANES), F32),
            vmem((n, 1, LANES), jnp.int32),
            vmem((n, 1, LANES), jnp.int32),
            pltpu.SMEM((n, 1, LANES), jnp.int32),
            vmem((n, packet, LANES), BF16),
            vmem((2, n, packet, LANES), BF16),
            vmem((half, LANES), jnp.int32),
            vmem((half, 3 * LANES), F32),
            vmem((half, predictors.shape[1]), BF16),
            vmem((chan, count), BF16),
            vmem((1, chan), F32),
            vmem(w_col.shape, BF16),
            vmem(w_col.shape, BF16),
            vmem(w_pred.shape, BF16),
            vmem(w_pred.shape, BF16),
            vmem(w_mid.shape, BF16),
            vmem(w_mid.shape, BF16),
            vmem(w_out.shape, BF16),
            vmem(w_out.shape, BF16),
            vmem((LANES, hid), F32),
            vmem((LANES + w_pred.shape[0], hid), BF16),
            vmem((LANES + w_pred.shape[0], hid), BF16),
            vmem((2, chan, half // 2), F32),
            vmem((2, chan, half // 2), F32),
            dma((9,)),
            dma((n,)), dma((n,)), dma((n,)), dma((n,)), dma((n,)), dma((n,)),
            dma((4,)), dma((4,)),
            dma((2,)), dma((2,)),
            dma,
        ],
        compiler_params=pltpu.CompilerParams(
            collective_id=0, has_side_effects=True, vmem_limit_bytes=60 * 1024 * 1024
        ),
    )(
        cells.reshape(1, count), predictors, observed.T, obs_error.reshape(1, chan), columns.T,
        w_col, w_pred, w_mid, w_out,
    ).T


def solution(mesh):
    return jax.shard_map(
        on_device,
        mesh=mesh,
        in_specs=(
            P("obs", "chan"),
            P("obs", None),
            P("obs"),
            P("obs", None),
            P("chan"),
            P(None, "chan"),
            P(None, "chan"),
            P(None, "chan"),
            P("chan", None),
        ),
        out_specs=P("obs", "chan"),
        check_vma=False,
    )
```

time: 121 us -> 40.3 us (0.33)
  the two profiles are of different devices: /device:TPU:0 before, /device:TPU:25 now
where the time goes in v1:
time: 40.3 us; the launch traced here: 40.2 us
  Pallas kernels  38.5 us (96%)
  local copies, waits for them, and re-layouts  1.67 us (4%)
    pallas_call x1, Pallas kernels, on_device(): pl.pallas_call(functools.partial(kernel, n, slots), out_shape=jax.ShapeDt...  38.5 us
    unnamed x1, local copies, waits for them, and re-layouts  1.67 us

profile of v1, /device:TPU:25, one launch (start us, length us, event | category | flops | bytes accessed | tf_op | source)
XLA Modules:
  0.0 40.2 jit_solution(9296125928751588621)
XLA Ops:
  0.0 38.5 %shard_map.91 = f32[64,1024]{1,0:T(8,128)} custom-call(s32[1,1024]{1,0:T(1,128)} %bitcast.8, bf16[1024,128]{1,0:T(8,128)(2,1)} %pred_.1, bf16[64,1024]{1,0:T(8,128)(2,1)} %bitcast.7, f32[1,64]{1,0:T(1,128)} %bitcast.9, bf16[274,4096]{1,0:T(8,128)(2,1)} %bitcast.5, bf16[274,512]{1,0:T(8,128)(2,1)} %wc.1, bf16[128,512]{1,0:T(8,128)(2,1)} %wp.1, ...), custom_call_target="tpu_custom_call" | custom-call | tf_op jit(solution)/shard_map/pallas_call | solution.py:318
  38.5 1.7 %copy.11 = f32[1024,64]{0,1:T(8,128)} copy(f32[1024,64]{0,1:T(8,128)} %bitcast.6) | data formatting | bytes 524288

commit v2 on v1

--- a/solution.py
+++ b/solution.py
@@ -195,8 +195,13 @@
             device_id_type=MESH,
         )
 
+    def turn_of(j):
+        far = n // 2 + (2 * (j & 1) - 1) * (j >> 1)
+        return jnp.where(j == 0, 0, far)
+
     @pl.loop(1, n)
-    def _(t):
+    def _(j):
+        t = turn_of(j)
         asker = lax.rem(me + t, n)
         gather(asker, sendbuf.at[asker])
         col_copy(t).start()
@@ -218,39 +223,53 @@
         swap.wait()
     tail(wc_oth, wp_oth, w2_oth)
 
-    def place_rows(t):
-        o = lax.rem(me + n - t, n)
-        forward(t).wait_recv()
+    batch = 4
+
+    def place_rows(g):
         sides = []
-        for s in range(2):
-            packed = recv[s, o, 2 * slots : 2 * slots + 16, :].astype(F32)
-            rest = [packed] + [pltpu.roll(packed, LANES - PACK * j, 1) for j in range(1, groups)]
-            sides.append(
-                jnp.concatenate(
-                    [
-                        recv[s, o, 0:slots, :],
-                        recv[s, o, slots : 2 * slots, :],
-                        jnp.concatenate(rest, axis=0).astype(BF16),
-                    ],
-                    axis=1,
+        slot = lax.broadcasted_iota(jnp.int32, (8, batch * 2 * slots), 1)
+        wanted = slot
+        for i in range(batch):
+            t = turn_of(g * batch + i)
+            o = lax.rem(me + n - t, n)
+            forward(t).wait_recv()
+            wanted = jnp.where(slot >= i * 2 * slots, slot + (o - i) * (2 * slots), wanted)
+            for s in range(2):
+                packed = recv[s, o, 2 * slots : 2 * slots + 16, :].astype(F32)
+                rest = [packed]
+                rest += [pltpu.roll(packed, LANES - PACK * j, 1) for j in range(1, groups)]
+                sides.append(
+                    jnp.concatenate(
+                        [
+                            recv[s, o, 0:slots, :],
+                            recv[s, o, slots : 2 * slots, :],
+                            jnp.concatenate(rest, axis=0).astype(BF16),
+                        ],
+                        axis=1,
+                    )
                 )
-            )
         data = jnp.concatenate(sides, axis=0)
-        want = tcol[...] - o * (2 * slots)
-        lane = lax.broadcasted_iota(jnp.int32, (half, LANES), 1)
         pick = [
-            (want == lane + b).astype(F32).astype(BF16)[:, : min(LANES, 2 * slots - b)]
-            for b in range(0, 2 * slots, LANES)
+            (tcol[...] == wanted[0:1, b : b + LANES]).astype(F32).astype(BF16)
+            for b in range(0, batch * 2 * slots, LANES)
         ]
         acc[...] += dot(jnp.concatenate(pick, axis=1), data)
 
-    @pl.loop(1, n)
-    def _(t):
+    def pass_on(j):
+        t = turn_of(j)
         col_copy(t).wait_recv()
         forward(t).start()
-        place_rows(t - 1)
-
-    place_rows(n - 1)
+
+    for j in range(1, batch):
+        pass_on(j)
+
+    @pl.loop(1, n // batch)
+    def _(g):
+        for i in range(batch):
+            pass_on(g * batch + i)
+        place_rows(g - 1)
+
+    place_rows(n // batch - 1)
 
     parts = 2
     chunk = half // parts

time: 40.3 us -> 39.1 us (0.970)
  the two profiles are of different devices: /device:TPU:25 before, /device:TPU:0 now
where the time goes in v2:
time: 39.1 us; the launch traced here: 38.9 us
  Pallas kernels  37.2 us (95%)
  local copies, waits for them, and re-layouts  1.67 us (4%)
    pallas_call x1, Pallas kernels, on_device(): pl.pallas_call(functools.partial(kernel, n, slots), out_shape=jax.ShapeDt...  37.2 us
    unnamed x1, local copies, waits for them, and re-layouts  1.67 us

profile of v2, /device:TPU:0, one launch (start us, length us, event | category | flops | bytes accessed | tf_op | source)
XLA Modules:
  0.0 38.9 jit_solution(18064900184373568294)
XLA Ops:
  0.0 37.2 %shard_map.91 = f32[64,1024]{1,0:T(8,128)} custom-call(s32[1,1024]{1,0:T(1,128)} %bitcast.8, bf16[1024,128]{1,0:T(8,128)(2,1)} %pred_.1, bf16[64,1024]{1,0:T(8,128)(2,1)} %bitcast.7, f32[1,64]{1,0:T(1,128)} %bitcast.9, bf16[274,4096]{1,0:T(8,128)(2,1)} %bitcast.5, bf16[274,512]{1,0:T(8,128)(2,1)} %wc.1, bf16[128,512]{1,0:T(8,128)(2,1)} %wp.1, ...), custom_call_target="tpu_custom_call" | custom-call | tf_op jit(solution)/shard_map/pallas_call | solution.py:337
  37.2 1.7 %copy.11 = f32[1024,64]{0,1:T(8,128)} copy(f32[1024,64]{0,1:T(8,128)} %bitcast.6) | data formatting | bytes 524288
